TPU v7x, 32 devices: a whole 2x2x4 slice. The times are simulated.
32 devices in a mesh: expert: 4 (over z), tensor: 8 (over y, x, core).
Axes of the slice: x: 2, y: 2, z: 4, core: 2. Of those that a mesh axis runs over, the one named last changes fastest.
Arguments:
- activations: bfloat16 [3072, 512], P('tensor', 'expert'), may hold values from -6 to 6
- cotangent: bfloat16 [3072, 512], P('tensor', 'expert'), may hold values from -4 to 4
- route_ids: int32 [512, 2], P('expert'), may hold values from 0 to 3, all different within a row; in each aligned block of 128 rows (0 to 127, 128 to 255, ...) at most 80 rows name the same one
- gate_probs: float32 [512, 2], P('expert'), may hold values from 0.2 to 0.8
- gate_weight: bfloat16 [4, 3072, 16384], P('expert', None, 'tensor'), may hold values from -0.15625 to 0.15625
- up_weight: bfloat16 [4, 3072, 16384], P('expert', None, 'tensor'), may hold values from -0.15625 to 0.15625
- down_weight: bfloat16 [4, 16384, 3072], P('expert', 'tensor'), may hold values from -0.046875 to 0.046875
Outputs:
- grad_input: bfloat16 [3072, 512], P('tensor', 'expert')
- score_grad: float32 [512, 2], P('expert')
Inputs may be any that keep to these rules, and one draw needn't show every extreme that they name: `route_ids`: each token names 2 different experts. Among the 128 tokens of one index of the expert axis no expert is named more than 80 times, and in every draw some such block names one expert exactly 80 times.
All inputs are finite; a program needn't handle non-finite values.
Results may differ from a plain program's by a relative error of at most 0.008.
Values may be sent and summed in bfloat16 or wider, within the bound.
A program may use at most 128 MiB of HBM per device.

v0:
```python
import jax
import jax.numpy as jnp
from jax import lax
from jax.sharding import PartitionSpec as P


def slot_numbers(route_ids, expert_count, capacity):
    token_count = route_ids.shape[0]
    onehot = (
        route_ids[:, :, None] == jnp.arange(expert_count, dtype=jnp.int32)[None, None, :]
    ).astype(jnp.int32)
    flattened = onehot.reshape(token_count * route_ids.shape[1], expert_count)
    earlier = jnp.cumsum(flattened, axis=0) - flattened
    position = jnp.sum(earlier * flattened, axis=1).reshape(route_ids.shape)
    return route_ids * capacity + position


def swiglu_backward(gate_sum, up_sum, hidden_grad):
    sigma = jax.nn.sigmoid(gate_sum)
    silu_value = gate_sum * sigma
    grad_up = (hidden_grad * silu_value).astype(jnp.bfloat16)
    grad_gate = (hidden_grad * up_sum * sigma * (1.0 + gate_sum * (1.0 - sigma))).astype(
        jnp.bfloat16
    )
    score_rows = jnp.sum(silu_value * up_sum * hidden_grad, axis=1)
    return (grad_gate, grad_up, score_rows)


def body(activations, cotangent, route_ids, gate_probs, gate_weight, up_weight, down_weight):
    expert_count = lax.axis_size("expert")
    tokens_here = route_ids.shape[0]
    capacity = min(tokens_here, 5 * tokens_here // (2 * expert_count))
    slot_total = expert_count * capacity
    destination = slot_numbers(route_ids, expert_count, capacity)
    slot_range = jnp.arange(slot_total, dtype=jnp.int32)
    matches = destination[:, :, None] == slot_range[None, None, :]
    placing = jnp.sum(matches.astype(jnp.float32), axis=1).astype(jnp.bfloat16)
    weighting = jnp.sum(jnp.where(matches, gate_probs[:, :, None], jnp.float32(0.0)), axis=1)
    gate_local = gate_weight[0]
    up_local = up_weight[0]
    down_local = down_weight[0]
    first_dims = (((0,), (0,)), ((), ()))
    down_dims = (((0,), (1,)), ((), ()))
    hidden_dims = (((1,), (1,)), ((), ()))
    send_in = jnp.dot(activations, placing, preferred_element_type=jnp.float32).astype(jnp.bfloat16)
    send_grad = jnp.dot(cotangent, placing, preferred_element_type=jnp.float32).astype(jnp.bfloat16)
    recv_in, recv_grad = (
        lax.all_to_all(send_in, "expert", split_axis=1, concat_axis=1, tiled=True),
        lax.all_to_all(send_grad, "expert", split_axis=1, concat_axis=1, tiled=True),
    )
    feature_piece = lax.all_gather(recv_in, "tensor", axis=0, tiled=True)
    grad_piece = lax.all_gather(recv_grad, "tensor", axis=0, tiled=True)
    gate_rows = gate_local
    up_rows = up_local
    gate_sum = lax.dot_general(
        feature_piece, gate_rows, first_dims, preferred_element_type=jnp.float32
    )
    up_sum = lax.dot_general(feature_piece, up_rows, first_dims, preferred_element_type=jnp.float32)
    hidden_grad = lax.dot_general(
        grad_piece, down_local, down_dims, preferred_element_type=jnp.float32
    )
    gate_sum, up_sum, hidden_grad = (gate_sum, up_sum, hidden_grad)
    grad_gate, grad_up, score_rows = swiglu_backward(gate_sum, up_sum, hidden_grad)
    gate_rows = gate_local
    up_rows = up_local
    term = lax.dot_general(gate_rows, grad_gate, hidden_dims, preferred_element_type=jnp.float32)
    term_slice = lax.psum_scatter(
        term + lax.dot_general(up_rows, grad_up, hidden_dims, preferred_element_type=jnp.float32),
        "tensor",
        scatter_dimension=0,
        tiled=True,
    )
    score_whole = lax.psum(score_rows[None, :], "tensor")
    back_terms, back_scores = (
        lax.all_to_all(term_slice, "expert", split_axis=1, concat_axis=1, tiled=True),
        lax.all_to_all(score_whole, "expert", split_axis=1, concat_axis=1, tiled=True),
    )
    grad_local = jnp.dot(
        back_terms, weighting.T, precision=lax.Precision.HIGHEST, preferred_element_type=jnp.float32
    )
    score_grad = jnp.sum(
        jnp.where(matches, back_scores[0][None, None, :], jnp.float32(0.0)), axis=2
    )
    grad_input = grad_local.astype(jnp.bfloat16)
    return (grad_input, score_grad)


def solution(mesh):
    in_specs = (
        P("tensor", "expert"),
        P("tensor", "expert"),
        P("expert", None),
        P("expert", None),
        P("expert", None, "tensor"),
        P("expert", None, "tensor"),
        P("expert", "tensor", None),
    )
    out_specs = (P("tensor", "expert"), P("expert", None))
    return jax.shard_map(body, mesh=mesh, in_specs=in_specs, out_specs=out_specs, check_vma=False)
```

profile of v0, /device:TPU:0, one launch (start us, length us, event | category | flops | bytes accessed | tf_op | source)
XLA Modules:
  0.0 196.6 jit_solution(7159178132124961180)
XLA Ops:
  7.2 0.8 copy.34
  8.0 0.1 eq.43
  8.2 0.1 eq.39
  8.3 1.2 reduce-window.6
  9.5 0.1 slice.8
  9.6 0.1 copy.36
  9.8 0.1 copy.37
  9.9 0.1 add_bitcast_fusion
  9.9 0.1 reshape.38
  10.2 0.7 multiply_add_fusion
  10.9 0.2 convolution_convert_fusion
  11.2 14.7 %all_to_all.45 = bf16[384,4,80]{0,2,1:T(8,128)(2,1)} all-to-all(bf16[384,4,80]{0,2,1:T(8,128)(2,1)S(1)} %bitcast.64), channel_id=1, replica_groups=mesh['expert'=4,'tensor'=8] {'expert'}, dimensions={1} | all-to-all | bytes 491520 | tf_op jit(solution)/shard_map/all_to_all | solution.py:48
  26.0 1.1 convolution_convert_fusion.1
  27.1 10.7 %all_to_all.46 = bf16[384,4,80]{0,2,1:T(8,128)(2,1)} all-to-all(bf16[384,4,80]{0,2,1:T(8,128)(2,1)S(1)} %bitcast.63), channel_id=1, replica_groups=mesh['expert'=4,'tensor'=8] {'expert'}, dimensions={1} | all-to-all | bytes 491520 | tf_op jit(solution)/shard_map/all_to_all | solution.py:49
  37.9 14.9 %all-gather.5.cloned.1.call-done = bf16[3072,320]{0,1:T(8,128)(2,1)} async-done(((bf16[384,320]{0,1:T(8,128)(2,1)}), bf16[3072,320]{0,1:T(8,128)(2,1)}) %all-gather.5.cloned.1.call-update) | async-done | bytes 1966096 | tf_op jit(solution)/shard_map/all_gather | solution.py:51
  52.8 9.4 %fusion.2 = f32[320,2048]{1,0:T(8,128)S(1)} fusion(bf16[3072,320]{0,1:T(8,128)(2,1)} %all-gather.5.cloned.1.call-done, bf16[1,3072,2048]{2,1,0:T(8,128)(2,1)} %param.11), kind=kOutput, calls=%fused_computation.2 | convolution fusion | flops 4026531840 | bytes 17170432 | tf_op jit(solution)/shard_map/dot_general | solution.py:55
  62.2 8.9 %fusion.6 = f32[320,2048]{1,0:T(8,128)} fusion(bf16[3072,320]{0,1:T(8,128)(2,1)S(1)} %copy-done.2, bf16[1,3072,2048]{2,1,0:T(8,128)(2,1)} %param.12), kind=kOutput, calls=%fused_computation.6 | convolution fusion | flops 4026531840 | bytes 17170432 | tf_op jit(solution)/shard_map/dot_general | solution.py:58
  71.1 11.3 %all-gather.3.cloned.1.call-done = bf16[3072,320]{0,1:T(8,128)(2,1)} async-done(((bf16[384,320]{0,1:T(8,128)(2,1)}), bf16[3072,320]{0,1:T(8,128)(2,1)}) %all-gather.3.cloned.1.call-update) | async-done | bytes 1966096 | tf_op jit(solution)/shard_map/all_gather | solution.py:52
  82.3 12.0 %multiply_reduce_fusion = (f32[320]{0:T(512)S(1)}, f32[320,2048]{1,0:T(8,128)}) fusion(f32[320,2048]{1,0:T(8,128)} %fusion.6, f32[320,2048]{1,0:T(8,128)S(1)} %fusion.2, bf16[3072,320]{0,1:T(8,128)(2,1)} %all-gather.3.cloned.1.call-done, bf16[1,2048,3072]{2,1,0:T(8,128)(2,1)} %param.13), kind=kOutput, calls=%fused_computation.12 | convolution fusion | flops 4031119104 | bytes 22414592 | tf_op jit(solution)/shard_map/dot_general | solution.py:59
  94.3 12.7 %fusion = f32[320,3072]{1,0:T(8,128)} fusion(bf16[1,3072,2048]{2,1,0:T(8,128)(2,1)} %param.11, f32[320,2048]{1,0:T(8,128)S(1)} %fusion.2, f32[320,2048]{1,0:T(8,128)} %get-tuple-element.5, f32[320,2048]{1,0:T(8,128)} %fusion.6), kind=kOutput, calls=%fused_computation | convolution fusion | flops 4033085440 | bytes 24379392 | tf_op jit(solution)/shard_map/dot_general | solution.py:66
  107.0 12.6 %fusion.13 = f32[3072,320]{0,1:T(8,128)} fusion(f32[320,3072]{1,0:T(8,128)} %fusion, bf16[1,3072,2048]{2,1,0:T(8,128)(2,1)} %param.12, f32[320,2048]{1,0:T(8,128)} %get-tuple-element.5, f32[320,2048]{1,0:T(8,128)S(1)} %fusion.2), kind=kOutput, calls=%fused_computation.11 | convolution fusion | flops 4031447040 | bytes 25690112 | tf_op jit(solution)/shard_map/dot_general | solution.py:68
  119.7 0.1 all_to_all.39
  119.8 13.1 %psum.7 = f32[1,4,80]{2,0,1:T(1,128)S(1)} all-reduce(f32[1,4,80]{2,0,1:T(1,128)S(1)} %all_to_all.39), channel_id=1, replica_groups=mesh['expert'=4,'tensor'=8] {'tensor'}, use_global_device_ids=true, to_apply=%region_7.8 | all-reduce | flops 320 | bytes 2560 | tf_op jit(solution)/shard_map/psum | solution.py:73
  132.9 9.9 %all_to_all.47 = f32[1,4,80]{2,0,1:T(1,128)S(1)} all-to-all(f32[1,4,80]{2,0,1:T(1,128)S(1)} %psum.7), channel_id=1, replica_groups=mesh['expert'=4,'tensor'=8] {'expert'}, dimensions={1} | all-to-all | bytes 2560 | tf_op jit(solution)/shard_map/all_to_all | solution.py:76
  142.8 27.1 %reduce-scatter.2.cloned.1.call-done = f32[384,320]{0,1:T(8,128)} async-done(((f32[3072,320]{0,1:T(8,128)}), f32[384,320]{0,1:T(8,128)}) %reduce-scatter.2.cloned.1.call-update) | async-done | bytes 491536 | tf_op jit(solution)/shard_map/reduce_scatter | solution.py:67
  169.9 4.6 %all-to-all-start.2 = ((f32[384,4,80]{0,2,1:T(8,128)}), f32[384,4,80]{0,2,1:T(8,128)S(1)}, u32[]{:S(2)}, u32[]{:S(2)}) async-start(f32[384,4,80]{0,2,1:T(8,128)} %bitcast.65), calls=%async_computation.3 | async-start | bytes 983040 | tf_op jit(solution)/shard_map/all_to_all | solution.py:75
  174.5 0.5 broadcast.35
  175.0 0.7 reduce.3
  175.7 0.1 broadcast_in_dim.35
  175.7 0.7 select_reduce_fusion
  176.4 11.8 %all-to-all-done.2 = f32[384,4,80]{0,2,1:T(8,128)S(1)} async-done(((f32[384,4,80]{0,2,1:T(8,128)}), f32[384,4,80]{0,2,1:T(8,128)S(1)}, u32[]{:S(2)}, u32[]{:S(2)}) %all-to-all-start.2) | async-done | bytes 491552 | tf_op jit(solution)/shard_map/all_to_all | solution.py:75
  188.3 1.8 convolution_convert_fusion.2
  (18 shorter events, 0.4 us)
Async XLA Ops:
  7.2 3.7 %copy-start = (bf16[384,128]{1,0:T(8,128)(2,1)S(1)}, bf16[384,128]{1,0:T(8,128)(2,1)}, u32[]{:S(2)}) copy-start(bf16[384,128]{1,0:T(8,128)(2,1)} %param.7) | copy-start | bytes 294916
  7.2 45.6 %all-gather.5.cloned.1.call-start = ((), (), s32[]{:S(2)}) async-start(), calls=%async_computation.6 | async-start | bytes 2211840 | tf_op jit(solution)/shard_map/all_gather | solution.py:51
  25.9 56.4 %all-gather.3.cloned.1.call-start = ((), (), s32[]{:S(2)}) async-start(), calls=%async_computation.5 | async-start | bytes 2211840 | tf_op jit(solution)/shard_map/all_gather | solution.py:52
  37.9 132.0 %reduce-scatter.2.cloned.1.call-start = ((), (), s32[]{:S(2)}) async-start(), calls=%async_computation.7 | async-start | bytes 4423680 | tf_op jit(solution)/shard_map/reduce_scatter | solution.py:67
  52.8 9.4 %copy-start.2 = (bf16[3072,320]{0,1:T(8,128)(2,1)S(1)}, bf16[3072,320]{0,1:T(8,128)(2,1)}, u32[]{:S(2)}) copy-start(bf16[3072,320]{0,1:T(8,128)(2,1)} %all-gather.5.cloned.1.call-done) | copy-start | bytes 5898244
  119.7 56.1 %copy-start.1 = (f32[128,2]{0,1:T(2,128)S(1)}, f32[128,2]{0,1:T(2,128)}, u32[]{:S(2)}) copy-start(f32[128,2]{0,1:T(2,128)} %param.10) | copy-start | bytes 3076
  169.9 18.4 %all-to-all-start.2 = ((f32[384,4,80]{0,2,1:T(8,128)}), f32[384,4,80]{0,2,1:T(8,128)S(1)}, u32[]{:S(2)}, u32[]{:S(2)}) async-start(f32[384,4,80]{0,2,1:T(8,128)} %bitcast.65), calls=%async_computation.3 | async-start | bytes 983040 | tf_op jit(solution)/shard_map/all_to_all | solution.py:75
Sparse Core Ops, SparseCore 0:
  26.1 26.7 all-gather.4
  54.7 27.6 all-gather.2
  119.8 50.0 reduce-scatter.1
where the time goes:
time: 197 us
  waiting for transfers between devices  65.1 us (33%)
  matrix products  58.7 us (30%)
  blocking collectives  48.5 us (25%)
  between operations  13.8 us (7%)
  starting transfers between devices  4.72 us (2%)
  other arithmetic  3.47 us (2%)
  local copies, waits for them, and re-layouts  2.24 us (1%)
    reduce_scatter x1, waiting for transfers between devices, body(): lax.psum_scatter(term + lax.dot_general(up_rows, grad_up, hidden_dims, pr...  27.1 us
    all_gather x1, waiting for transfers between devices, body(): feature_piece = lax.all_gather(recv_in, 'tensor', axis=0, tiled=True)  14.9 us
    all_to_all x1, blocking collectives, body(): lax.all_to_all(send_in, 'expert', split_axis=1, concat_axis=1, tiled=True)  14.7 us
    psum x1, blocking collectives, body(): score_whole = lax.psum(score_rows[None, :], 'tensor')  13.1 us
    dot_general x1, matrix products, body(): lax.dot_general(gate_rows, grad_gate, hidden_dims, preferred_element_type...  12.7 us
    dot_general x1, matrix products, body(): lax.dot_general(up_rows, grad_up, hidden_dims, preferred_element_type=jnp...  12.6 us
    dot_general x1, matrix products, body(): lax.dot_general(grad_piece, down_local, down_dims, preferred_element_type...  12 us
    all_to_all x1, waiting for transfers between devices, body(): lax.all_to_all(term_slice, 'expert', split_axis=1, concat_axis=1, tiled=T...  11.8 us
  transfers between devices with their start and end apart: 4, of which 4 were waited for; matrix products, arithmetic and copies ran while one was open for 11% of the time, Pallas kernels for 0%

commit v1 on v0

--- a/solution.py
+++ b/solution.py
@@ -48,8 +48,11 @@
         lax.all_to_all(send_in, "expert", split_axis=1, concat_axis=1, tiled=True),
         lax.all_to_all(send_grad, "expert", split_axis=1, concat_axis=1, tiled=True),
     )
-    feature_piece = lax.all_gather(recv_in, "tensor", axis=0, tiled=True)
-    grad_piece = lax.all_gather(recv_grad, "tensor", axis=0, tiled=True)
+    feature_piece, grad_piece = jnp.split(
+        lax.all_gather(jnp.concatenate([recv_in, recv_grad], axis=1), "tensor", axis=0, tiled=True),
+        [recv_in.shape[1]],
+        axis=1,
+    )
     gate_rows = gate_local
     up_rows = up_local
     gate_sum = lax.dot_general(

time: 197 us -> 206 us (1.046)
  waiting for transfers between devices: 65.1 us -> 81.9 us
  blocking collectives: 48.5 us -> 33.3 us
  starting transfers between devices: 4.72 us -> 11 us
    all_to_all x1 -> x0, blocking collectives: 14.7 us -> none  [body(): lax.all_to_all(send_in, 'expert', split_axis=1, concat_axis=1, tiled=True)]
    all_gather x2 -> x1, waiting for transfers between devices: 26.2 us -> 35.5 us  [body(): lax.all_gather(jnp.concatenate([recv_in, recv_grad], axis=1), 'tensor', a...]
    all_to_all x0 -> x1, waiting for transfers between devices: none -> 7.43 us  [body(): lax.all_to_all(send_in, 'expert', split_axis=1, concat_axis=1, tiled=True)]
    all_to_all x0 -> x1, starting transfers between devices: none -> 6.31 us  [body(): lax.all_to_all(send_in, 'expert', split_axis=1, concat_axis=1, tiled=True)]
  transfers between devices with their start and end apart: 4 -> 4, of which waited for: 4 -> 4; matrix products, arithmetic and copies ran while one was open for 11% -> 2% of each run, Pallas kernels for 0% -> 0%
where the time goes in v1:
time: 206 us; the launch traced here: 205 us
  waiting for transfers between devices  81.9 us (40%)
  matrix products  58.3 us (28%)
  blocking collectives  33.3 us (16%)
  between operations  14.1 us (7%)
  starting transfers between devices  11 us (5%)
  other arithmetic  4.29 us (2%)
  local copies, waits for them, and re-layouts  2.28 us (1%)
    all_gather x1, waiting for transfers between devices, body(): lax.all_gather(jnp.concatenate([recv_in, recv_grad], axis=1), 'tensor', a...  35.5 us
    reduce_scatter x1, waiting for transfers between devices, body(): lax.psum_scatter(term + lax.dot_general(up_rows, grad_up, hidden_dims, pr...  27.1 us
    psum x1, blocking collectives, body(): score_whole = lax.psum(score_rows[None, :], 'tensor')  13.1 us
    dot_general x1, matrix products, body(): lax.dot_general(gate_rows, grad_gate, hidden_dims, preferred_element_type...  12.7 us
    dot_general x1, matrix products, body(): lax.dot_general(up_rows, grad_up, hidden_dims, preferred_element_type=jnp...  12.6 us
    dot_general x1, matrix products, body(): lax.dot_general(grad_piece, down_local, down_dims, preferred_element_type...  12.3 us
    all_to_all x1, waiting for transfers between devices, body(): lax.all_to_all(term_slice, 'expert', split_axis=1, concat_axis=1, tiled=T...  11.8 us
    all_to_all x1, blocking collectives, body(): lax.all_to_all(send_grad, 'expert', split_axis=1, concat_axis=1, tiled=True)  10.3 us
  transfers between devices with their start and end apart: 4, of which 4 were waited for; matrix products, arithmetic and copies ran while one was open for 2% of the time, Pallas kernels for 0%

profile of v1, /device:TPU:0, one launch (start us, length us, event | category | flops | bytes accessed | tf_op | source)
XLA Modules:
  0.0 205.1 jit_solution(8976297921016044334)
XLA Ops:
  7.2 0.8 copy.34
  8.0 0.1 eq.43
  8.1 0.1 eq.39
  8.3 1.2 reduce-window.6
  9.5 0.1 slice.8
  9.6 0.1 copy.36
  9.7 0.1 copy.37
  9.9 0.1 reshape.38
  10.1 0.7 multiply_add_fusion
  10.9 0.9 convolution_convert_fusion.1
  11.8 6.3 %all-to-all-start = ((bf16[384,4,80]{0,2,1:T(8,128)(2,1)}), bf16[384,4,80]{0,2,1:T(8,128)(2,1)S(1)}, u32[]{:S(2)}, u32[]{:S(2)}) async-start(bf16[384,4,80]{0,2,1:T(8,128)(2,1)} %bitcast.3), calls=%async_computation | async-start | bytes 491520 | tf_op jit(solution)/shard_map/all_to_all | solution.py:48
  18.1 1.1 convolution_convert_fusion
  19.3 7.4 %all-to-all-done = bf16[384,4,80]{0,2,1:T(8,128)(2,1)S(1)} async-done(((bf16[384,4,80]{0,2,1:T(8,128)(2,1)}), bf16[384,4,80]{0,2,1:T(8,128)(2,1)S(1)}, u32[]{:S(2)}, u32[]{:S(2)}) %all-to-all-start) | async-done | bytes 245792 | tf_op jit(solution)/shard_map/all_to_all | solution.py:48
  26.7 10.3 %all_to_all.45 = bf16[384,4,80]{0,2,1:T(8,128)(2,1)S(1)} all-to-all(bf16[384,4,80]{0,2,1:T(8,128)(2,1)S(1)} %bitcast.58), channel_id=1, replica_groups=mesh['expert'=4,'tensor'=8] {'expert'}, dimensions={1} | all-to-all | bytes 491520 | tf_op jit(solution)/shard_map/all_to_all | solution.py:49
  37.0 0.8 pad_maximum_fusion
  37.9 35.5 %all-gather.2.cloned.1.call-done = bf16[3072,640]{0,1:T(8,128)(2,1)} async-done(((bf16[384,640]{0,1:T(8,128)(2,1)}), bf16[3072,640]{0,1:T(8,128)(2,1)}) %all-gather.2.cloned.1.call-update) | async-done | bytes 3932176 | tf_op jit(solution)/shard_map/all_gather | solution.py:52
  73.4 9.4 %fusion.2 = f32[320,2048]{1,0:T(8,128)S(1)} fusion(bf16[1,3072,2048]{2,1,0:T(8,128)(2,1)} %param.11, bf16[3072,640]{0,1:T(8,128)(2,1)} %all-gather.2.cloned.1.call-done), kind=kOutput, calls=%fused_computation.2 | convolution fusion | flops 4026531840 | bytes 17170432 | tf_op jit(solution)/shard_map/dot_general | solution.py:58
  82.8 7.4 %fusion.6 = f32[320,2048]{1,0:T(8,128)S(1)} fusion(bf16[1,3072,2048]{2,1,0:T(8,128)(2,1)} %param.12, bf16[3072,640]{0,1:T(8,128)(2,1)S(1)} %copy-done.2), kind=kOutput, calls=%fused_computation.6 | convolution fusion | flops 4026531840 | bytes 17170432 | tf_op jit(solution)/shard_map/dot_general | solution.py:61
  90.3 12.3 %multiply_reduce_fusion = (f32[320]{0:T(512)S(1)}, f32[320,2048]{1,0:T(8,128)}) fusion(f32[320,2048]{1,0:T(8,128)S(1)} %fusion.6, f32[320,2048]{1,0:T(8,128)S(1)} %fusion.2, bf16[1,2048,3072]{2,1,0:T(8,128)(2,1)} %param.13, bf16[3072,640]{0,1:T(8,128)(2,1)} %all-gather.2.cloned.1.call-done), kind=kOutput, calls=%fused_computation.12 | convolution fusion | flops 4031119104 | bytes 22414592 | tf_op jit(solution)/shard_map/dot_general | solution.py:62
  102.6 12.7 %fusion = f32[320,3072]{1,0:T(8,128)} fusion(bf16[1,3072,2048]{2,1,0:T(8,128)(2,1)} %param.11, f32[320,2048]{1,0:T(8,128)S(1)} %fusion.2, f32[320,2048]{1,0:T(8,128)} %get-tuple-element.5, f32[320,2048]{1,0:T(8,128)} %copy-done.3), kind=kOutput, calls=%fused_computation | convolution fusion | flops 4033085440 | bytes 24379392 | tf_op jit(solution)/shard_map/dot_general | solution.py:69
  115.3 12.6 %fusion.13 = f32[3072,320]{0,1:T(8,128)} fusion(f32[320,3072]{1,0:T(8,128)} %fusion, bf16[1,3072,2048]{2,1,0:T(8,128)(2,1)} %param.12, f32[320,2048]{1,0:T(8,128)} %get-tuple-element.5, f32[320,2048]{1,0:T(8,128)S(1)} %fusion.2), kind=kOutput, calls=%fused_computation.11 | convolution fusion | flops 4031447040 | bytes 25690112 | tf_op jit(solution)/shard_map/dot_general | solution.py:71
  128.0 0.1 all_to_all.39
  128.0 13.1 %psum.7 = f32[1,4,80]{2,0,1:T(1,128)S(1)} all-reduce(f32[1,4,80]{2,0,1:T(1,128)S(1)} %all_to_all.39), channel_id=1, replica_groups=mesh['expert'=4,'tensor'=8] {'tensor'}, use_global_device_ids=true, to_apply=%region_7.8 | all-reduce | flops 320 | bytes 2560 | tf_op jit(solution)/shard_map/psum | solution.py:76
  141.1 9.9 %all_to_all.46 = f32[1,4,80]{2,0,1:T(1,128)S(1)} all-to-all(f32[1,4,80]{2,0,1:T(1,128)S(1)} %psum.7), channel_id=1, replica_groups=mesh['expert'=4,'tensor'=8] {'expert'}, dimensions={1} | all-to-all | bytes 2560 | tf_op jit(solution)/shard_map/all_to_all | solution.py:79
  151.1 27.1 %reduce-scatter.2.cloned.1.call-done = f32[384,320]{0,1:T(8,128)} async-done(((f32[3072,320]{0,1:T(8,128)}), f32[384,320]{0,1:T(8,128)}) %reduce-scatter.2.cloned.1.call-update) | async-done | bytes 491536 | tf_op jit(solution)/shard_map/reduce_scatter | solution.py:70
  178.1 4.6 %all-to-all-start.2 = ((f32[384,4,80]{0,2,1:T(8,128)}), f32[384,4,80]{0,2,1:T(8,128)S(1)}, u32[]{:S(2)}, u32[]{:S(2)}) async-start(f32[384,4,80]{0,2,1:T(8,128)} %bitcast.61), calls=%async_computation.3 | async-start | bytes 983040 | tf_op jit(solution)/shard_map/all_to_all | solution.py:78
  182.7 0.5 broadcast.35
  183.2 0.7 reduce.3
  183.9 0.1 broadcast_in_dim.35
  184.0 0.7 select_reduce_fusion
  184.7 11.8 %all-to-all-done.2 = f32[384,4,80]{0,2,1:T(8,128)S(1)} async-done(((f32[384,4,80]{0,2,1:T(8,128)}), f32[384,4,80]{0,2,1:T(8,128)S(1)}, u32[]{:S(2)}, u32[]{:S(2)}) %all-to-all-start.2) | async-done | bytes 491552 | tf_op jit(solution)/shard_map/all_to_all | solution.py:78
  196.5 1.8 convolution_convert_fusion.2
  (19 shorter events, 0.3 us)
Async XLA Ops:
  7.2 3.7 %copy-start = (bf16[384,128]{1,0:T(8,128)(2,1)S(1)}, bf16[384,128]{1,0:T(8,128)(2,1)}, u32[]{:S(2)}) copy-start(bf16[384,128]{1,0:T(8,128)(2,1)} %param.7) | copy-start | bytes 294916
  11.8 14.9 %all-to-all-start = ((bf16[384,4,80]{0,2,1:T(8,128)(2,1)}), bf16[384,4,80]{0,2,1:T(8,128)(2,1)S(1)}, u32[]{:S(2)}, u32[]{:S(2)}) async-start(bf16[384,4,80]{0,2,1:T(8,128)(2,1)} %bitcast.3), calls=%async_computation | async-start | bytes 491520 | tf_op jit(solution)/shard_map/all_to_all | solution.py:48
  18.1 55.2 %all-gather.2.cloned.1.call-start = ((), (), s32[]{:S(2)}) async-start(), calls=%async_computation.5 | async-start | bytes 4423680 | tf_op jit(solution)/shard_map/all_gather | solution.py:52
  37.8 140.3 %reduce-scatter.2.cloned.1.call-start = ((), (), s32[]{:S(2)}) async-start(), calls=%async_computation.6 | async-start | bytes 4423680 | tf_op jit(solution)/shard_map/reduce_scatter | solution.py:70
  73.4 9.4 %copy-start.2 = (bf16[3072,640]{0,1:T(8,128)(2,1)S(1)}, bf16[3072,640]{0,1:T(8,128)(2,1)}, u32[]{:S(2)}) copy-start(bf16[3072,640]{0,1:T(8,128)(2,1)} %all-gather.2.cloned.1.call-done) | copy-start | bytes 11796484
  90.3 12.3 %copy-start.3 = (f32[320,2048]{1,0:T(8,128)}, f32[320,2048]{1,0:T(8,128)S(1)}, u32[]{:S(2)}) copy-start(f32[320,2048]{1,0:T(8,128)S(1)} %fusion.6) | copy-start | bytes 7864324
  127.9 56.1 %copy-start.1 = (f32[128,2]{0,1:T(2,128)S(1)}, f32[128,2]{0,1:T(2,128)}, u32[]{:S(2)}) copy-start(f32[128,2]{0,1:T(2,128)} %param.10) | copy-start | bytes 3076
  178.1 18.4 %all-to-all-start.2 = ((f32[384,4,80]{0,2,1:T(8,128)}), f32[384,4,80]{0,2,1:T(8,128)S(1)}, u32[]{:S(2)}, u32[]{:S(2)}) async-start(f32[384,4,80]{0,2,1:T(8,128)} %bitcast.61), calls=%async_computation.3 | async-start | bytes 983040 | tf_op jit(solution)/shard_map/all_to_all | solution.py:78
Sparse Core Ops, SparseCore 0:
  38.0 35.3 all-gather.1
  128.1 50.0 reduce-scatter.1
